TPU v7x, 256 devices: a whole 4x4x8 slice. The times are simulated.
256 devices in a mesh: dp: 4 (over y), seq: 64 (over z, x, core).
Axes of the slice: x: 4, y: 4, z: 8, core: 2. Of those that a mesh axis runs over, the one named last changes fastest.
Arguments:
- query: bfloat16 [4, 16384, 1536], P('dp', 'seq'), may hold values from -6 to 6
- key: bfloat16 [4, 16384, 1536], P('dp', 'seq'), may hold values from -6 to 6
- value: bfloat16 [4, 16384, 1536], P('dp', 'seq'), may hold values from -6 to 6
- segments: int32 [4, 16384], P('dp', 'seq'), may hold values from 0 to 95, never falling along the last dimension, each value on 1 to 256 neighbouring positions
- out_proj: bfloat16 [1536, 1536], replicated, may hold values from -0.15625 to 0.15625
- conv_kernel: bfloat16 [31, 1536], replicated, may hold values from -1 to 1
- cotangent: bfloat16 [4, 16384, 1536], P('dp', 'seq'), may hold values from -6 to 6
Outputs:
- block_out: bfloat16 [4, 16384, 1536], P('dp', 'seq')
- grad_query: bfloat16 [4, 16384, 1536], P('dp', 'seq')
- grad_key: bfloat16 [4, 16384, 1536], P('dp', 'seq')
- grad_value: bfloat16 [4, 16384, 1536], P('dp', 'seq')
- grad_kernel: float32 [31, 1536], replicated
- grad_out_proj: float32 [1536, 1536], P(('dp', 'seq'))
Inputs may be any that keep to these rules, and one draw needn't show every extreme that they name: `segments`: along the frames of a data group the utterance number never falls; every utterance holds 1 to 256 frames and one holds exactly 256.
All inputs are finite; a program needn't handle non-finite values.
Results may differ from a plain program's by a relative error of at most 0.02.
Values may be sent and summed in bfloat16 or wider, within the bound.
No kernel may reach another device: no remote copies, remote signals or barrier semaphores. Data moves between devices by JAX's collectives and lax.ppermute only.
A program may use at most 128 MiB of HBM per device.

v0:
```python
import jax
import jax.numpy as jnp
from jax import lax
from jax.sharding import PartitionSpec as P

HD = 64
KW = 31


def extended(block, sides, width):
    for axis, dim in sides:
        count = lax.axis_size(axis)
        forward = [(i, i + 1) for i in range(count - 1)]
        backward = [(target, source) for source, target in forward]
        low = lax.ppermute(
            lax.slice_in_dim(block, block.shape[dim] - width, None, axis=dim), axis, forward
        )
        high = lax.ppermute(lax.slice_in_dim(block, 0, width, axis=dim), axis, backward)
        block = jnp.concatenate([low, block, high], axis=dim)
    return block


def from_behind(value, axis, steps):
    count = lax.axis_size(axis)
    first, last = (max(0, -steps), min(count, count - steps))
    return lax.ppermute(value, axis, [(source, source + steps) for source in range(first, last)])


def head_scores(queries, keys_block, query_ids, key_ids):
    query_heads = queries.reshape(queries.shape[0], -1, HD)
    key_heads = keys_block.reshape(keys_block.shape[0], -1, HD)
    scores = jnp.einsum(
        "rhe,whe->hrw", query_heads, key_heads, preferred_element_type=jnp.float32
    ) * HD ** (-0.5)
    allowed = query_ids[:, None] == key_ids[None, :]
    return jnp.where(allowed[None], scores, -1e30)


def to_groups(matrix):
    return jnp.moveaxis(matrix.reshape(matrix.shape[0], -1, 4 * HD), 1, 0)


def from_groups(stacked):
    return jnp.moveaxis(stacked, 0, 1).reshape(stacked.shape[1], -1)


def attend(queries, keys_block, values_block, query_ids, key_ids):
    scores = head_scores(queries, keys_block, query_ids, key_ids)
    highest = jnp.max(scores, axis=2)
    weights = jnp.exp(scores - highest[:, :, None])
    totals = jnp.sum(weights, axis=2)
    probs = (weights / totals[:, :, None]).astype(jnp.bfloat16)
    value_heads = values_block.reshape(values_block.shape[0], -1, HD)
    context = jnp.einsum("hrw,whe->rhe", probs, value_heads, preferred_element_type=jnp.float32)
    return (context.reshape(queries.shape[0], -1), highest, totals)


def score_grads(
    queries, keys_block, values_block, upstream, highest, totals, deltas, query_ids, key_ids
):
    scores = head_scores(queries, keys_block, query_ids, key_ids)
    probs = jnp.exp(scores - highest[:, :, None]) / totals[:, :, None]
    upstream_heads = upstream.reshape(upstream.shape[0], -1, HD)
    value_heads = values_block.reshape(values_block.shape[0], -1, HD)
    prob_grads = jnp.einsum(
        "rhe,whe->hrw", upstream_heads, value_heads, preferred_element_type=jnp.float32
    )
    score_grad = (probs * (prob_grads - deltas[:, :, None]) * HD ** (-0.5)).astype(jnp.bfloat16)
    return (probs.astype(jnp.bfloat16), score_grad, upstream_heads)


def query_side(queries, keys_block, score_grad):
    key_heads = keys_block.reshape(keys_block.shape[0], -1, HD)
    grads = jnp.einsum("hrw,whe->rhe", score_grad, key_heads, preferred_element_type=jnp.float32)
    return grads.reshape(queries.shape[0], -1)


def key_side(queries, keys_block, probs, score_grad, upstream_heads):
    query_heads = queries.reshape(queries.shape[0], -1, HD)
    key_part = jnp.einsum(
        "hrw,rhe->whe", score_grad, query_heads, preferred_element_type=jnp.float32
    )
    value_part = jnp.einsum(
        "hrw,rhe->whe", probs, upstream_heads, preferred_element_type=jnp.float32
    )
    return (key_part.reshape(keys_block.shape[0], -1), value_part.reshape(keys_block.shape[0], -1))


def per_device(query, key, value, segments, out_proj, conv_kernel, cotangent):
    frame_count = query.shape[1]
    width = query.shape[2]
    group_count = width // (4 * HD)
    reach = KW // 2
    queries = query[0]
    keys_local = key[0]
    values_local = value[0]
    own_ids = segments[0] + 1
    wide_ids = extended(own_ids, (("seq", 0),), frame_count)
    paired = extended(jnp.stack([keys_local, values_local]), (("seq", 1),), frame_count)

    def forward_group(items):
        return attend(items[0], items[1], items[2], own_ids, wide_ids)

    context_groups, highest, totals = lax.map(
        forward_group, (to_groups(queries), to_groups(paired[0]), to_groups(paired[1]))
    )
    context = from_groups(context_groups)
    context_b = context.astype(jnp.bfloat16)
    attended = jnp.dot(context_b, out_proj, preferred_element_type=jnp.float32).astype(jnp.bfloat16)
    attended_wide = extended(attended, (("seq", 0),), reach)
    conv_ids = wide_ids[frame_count - reach : 2 * frame_count + reach]
    kernel = conv_kernel.astype(jnp.float32)
    masks = [(conv_ids[offset : offset + frame_count] == own_ids)[:, None] for offset in range(KW)]
    convolved = jnp.zeros((frame_count, width), jnp.float32)
    for offset in range(KW):
        convolved = convolved + jnp.where(
            masks[offset],
            kernel[offset] * attended_wide[offset : offset + frame_count].astype(jnp.float32),
            0.0,
        )
    gate = jax.nn.sigmoid(convolved)
    block_out = (convolved * gate).astype(jnp.bfloat16)
    conv_grad = (cotangent[0].astype(jnp.float32) * gate * (1.0 + convolved * (1.0 - gate))).astype(
        jnp.bfloat16
    )
    conv_grad_wide = extended(conv_grad, (("seq", 0),), reach)
    conv_grad_f = conv_grad.astype(jnp.float32)
    attended_grad = jnp.zeros((frame_count, width), jnp.float32)
    kernel_rows = []
    for offset in range(KW):
        mirror = 2 * reach - offset
        attended_grad = attended_grad + jnp.where(
            masks[mirror],
            kernel[offset] * conv_grad_wide[mirror : mirror + frame_count].astype(jnp.float32),
            0.0,
        )
        kernel_rows.append(
            jnp.sum(
                jnp.where(
                    masks[offset],
                    conv_grad_f * attended_wide[offset : offset + frame_count].astype(jnp.float32),
                    0.0,
                ),
                axis=0,
            )
        )
    scale_out = (lax.axis_size("dp") * lax.axis_size("seq") * frame_count) ** (-0.5)
    grad_kernel = lax.psum(jnp.stack(kernel_rows), ("dp", "seq")) * scale_out
    attended_grad_b = attended_grad.astype(jnp.bfloat16)
    reduced = lax.psum_scatter(
        lax.dot_general(
            context_b, attended_grad_b, (((0,), (0,)), ((), ())), preferred_element_type=jnp.float32
        ),
        ("dp", "seq"),
        scatter_dimension=0,
        tiled=True,
    )
    grad_out_proj = reduced * scale_out
    context_grad = lax.dot_general(
        attended_grad_b, out_proj, (((1,), (1,)), ((), ())), preferred_element_type=jnp.float32
    ).astype(jnp.bfloat16)
    products = (to_groups(context_grad).astype(jnp.float32) * to_groups(context)).reshape(
        group_count, frame_count, 4, HD
    )
    deltas = jnp.moveaxis(jnp.sum(products, axis=3), 2, 1)

    def both_group(items):
        probs, score_grad, upstream_heads = score_grads(
            items[0], items[1], items[2], items[3], items[4], items[5], items[6], own_ids, wide_ids
        )
        key_part, value_part = key_side(items[0], items[1], probs, score_grad, upstream_heads)
        return (query_side(items[0], items[1], score_grad), key_part, value_part)

    query_part, key_part, value_part = lax.map(
        both_group,
        (
            to_groups(queries),
            to_groups(paired[0]),
            to_groups(paired[1]),
            to_groups(context_grad),
            highest,
            totals,
            deltas,
        ),
    )
    key_wide = from_groups(key_part)
    value_wide = from_groups(value_part)
    earlier = jnp.stack([key_wide[:frame_count], value_wide[:frame_count]])
    later = jnp.stack([key_wide[2 * frame_count :], value_wide[2 * frame_count :]])
    from_later = from_behind(earlier.astype(jnp.bfloat16), "seq", -1).astype(earlier.dtype)
    from_earlier = from_behind(later.astype(jnp.bfloat16), "seq", 1).astype(later.dtype)
    key_total = key_wide[frame_count : 2 * frame_count] + from_later[0] + from_earlier[0]
    value_total = value_wide[frame_count : 2 * frame_count] + from_later[1] + from_earlier[1]
    grad_query = from_groups(query_part).astype(jnp.bfloat16)
    grad_key = key_total.astype(jnp.bfloat16)
    grad_value = value_total.astype(jnp.bfloat16)
    return (
        block_out[None],
        grad_query[None],
        grad_key[None],
        grad_value[None],
        grad_kernel,
        grad_out_proj,
    )


def solution(mesh):
    in_specs = (
        P("dp", "seq", None),
        P("dp", "seq", None),
        P("dp", "seq", None),
        P("dp", "seq"),
        P(),
        P(),
        P("dp", "seq", None),
    )
    out_specs = (
        P("dp", "seq", None),
        P("dp", "seq", None),
        P("dp", "seq", None),
        P("dp", "seq", None),
        P(),
        P(("dp", "seq"), None),
    )
    return jax.shard_map(
        per_device, mesh=mesh, in_specs=in_specs, out_specs=out_specs, check_vma=False
    )
```

profile of v0, /device:TPU:1, one launch (start us, length us, event | category | flops | bytes accessed | tf_op | source)
XLA Modules:
  0.0 1732.6 jit_solution(641398557045694055)
XLA Ops:
  8.6 15.1 collective-permute-start.1
  30.7 13.3 collective-permute-start.3
  59.3 38.1 %while.30 = (s32[]{:T(128)}, f32[6,256,256]{1,2,0:T(8,128)}, f32[6,4,256]{2,1,0:T(4,128)}, f32[6,4,256]{2,1,0:T(4,128)}, bf16[6,768,256]{1,2,0:T(8,128)(2,1)S(1)...) while((s32[]{:T(128)}, f32[6,256,256]{1,2,0:T(8,128)}, ...), condition=%wide.region_3.4_spmd.clone, body=%wide.region_0.3_spmd.sunk.clone | while | flops 210958336 | bytes 13804649 | solution.py:104
  112.0 22.7 %fusion.142 = (f32[1536]{0:T(1024)}, f32[1536]{0:T(1024)}, f32[1536]{0:T(1024)}, f32[1536]{0:T(1024)}, f32[1536]{0:T(1024)}, /*index=5*/f32[1536]{0:T(1024)}, bf16[256,1536]{1,0:T(8,128)(2,1)S(1)}, f32[256,1536]{1,0:T(8,128)}) fusion(pred[256]{0:T(512)(128)(4,1)S(1)} %get-tuple-element.289, bf16[15,1536]{1,0:T(8,128)(2,1)S(1)} %collective-permute-done.5, ...), kind=kLoop, calls=%fused_computation.286 | loop fusion | flops 104193024 | bytes 4259328 | tf_op jit(solution)/shard_map/reduce_sum | solution.py:138
  142.5 24.2 %fusion.149 = bf16[256,1536]{1,0:T(8,128)(2,1)S(1)} fusion(bf16[256,1536]{1,0:T(8,128)(2,1)S(1)} %get-tuple-element.248, bf16[15,1536]{1,0:T(8,128)(2,1)} %collective-permute-done.7, bf16[15,1536]{1,0:T(8,128)(2,1)} %copy-done.74, f32[1536]{0:T(1024)S(1)} %get-tuple-element.174, f32[1536]{0:T(1024)S(1)} %get-tuple-element.175, ...), kind=kLoop, calls=%fused_computation.304 | loop fusion | flops 83755008 | bytes 1863168 | tf_op jit(solution)/shard_map/convert_element_type | solution.py:149
  171.8 723.4 %fusion = f32[8,1536]{1,0:T(8,128)S(1)} fusion(f32[1536,1536]{1,0:T(8,128)} %fusion.216), kind=kCustom, calls=%all-reduce-scatter | all-reduce-scatter fusion | flops 3145729 | bytes 9486336
  897.8 13.3 collective-permute-start.11
  930.9 13.1 collective-permute-start.13
  944.0 13.1 collective-permute-start.14
  957.2 13.1 collective-permute-start.15
  970.3 13.1 collective-permute-start.16
  1002.5 13.1 collective-permute-start.18
  1015.7 13.1 collective-permute-start.19
  1111.3 13.3 collective-permute-start.26
  1141.2 13.7 collective-permute-start.28
  1154.9 13.1 collective-permute-start.29
  1168.1 13.1 collective-permute-start.30
  1181.2 13.1 collective-permute-start.31
  1267.5 13.7 collective-permute-start.37
  1281.2 13.1 collective-permute-start.38
  1294.4 13.1 collective-permute-start.39
  1318.2 52.4 %while.31 = (s32[]{:T(128)}, bf16[6,256,256]{1,2,0:T(8,128)(2,1)S(1)}, f32[6,768,256]{1,2,0:T(8,128)}, f32[6,768,256]{1,2,0:T(8,128)}, bf16[6,768,256]{1,2,0:T(8...) while((s32[]{:T(128)}, ...), condition=%wide.region_6.7_spmd.clone, body=%wide.region_5.6_spmd.sunk.clone | while | flops 510590976 | bytes 23504016 | solution.py:174
  1489.9 96.9 %concatenate.118 = f32[518,1536]{1,0:T(8,128)} concatenate(f32[6,1536]{1,0:T(8,128)S(1)} %collective-permute-done.73, f32[8,1536]{1,0:T(8,128)} %collective-permute-done.72, f32[8,1536]{1,0:T(8,128)} %collective-permute-done.71, f32[8,1536]{1,0:T(8,128)} %collective-permute-done.70, f32[8,1536]{1,0:T(8,128)} %collective-permute-done.69, f32[8,1536]{1,0:T(8,128)} %collective-permute-done.68, ...), dimensions={0} | concatenate | bytes 6365184
  1588.4 128.7 %all-reduce.4.cloned.1.call-done = f32[31,1536]{1,0:T(8,128)} async-done(((f32[31,1536]{1,0:T(8,128)}), f32[31,1536]{1,0:T(8,128)}) %all-reduce.4.cloned.1.call-update) | async-done | bytes 190480 | tf_op jit(solution)/shard_map/psum | solution.py:148
  (664 shorter events, 491.5 us)
Async XLA Ops:
  7.2 1709.9 %all-reduce.4.cloned.1.call-start = ((), (), s32[]{:S(2)}) async-start(), calls=%async_computation | async-start | bytes 393216 | tf_op jit(solution)/shard_map/psum | solution.py:148
  897.8 72.5 %collective-permute-start.11 = (f32[8,1536]{1,0:T(8,128)S(1)}, f32[8,1536]{1,0:T(8,128)S(1)}, u32[]{:S(2)}, u32[]{:S(2)}) collective-permute-start(f32[8,1536]{1,0:T(8,128)S(1)} %fusion), channel_id=1, source_target_pairs={{0,2},{1,3},{2,4},{3,5},{4,6},{5,7},{6,8},{7,9},{8,10},{9,11},{10,... | collective-permute-start | bytes 147464
  917.8 71.6 %collective-permute-start.12 = (f32[8,1536]{1,0:T(8,128)S(1)}, f32[8,1536]{1,0:T(8,128)S(1)}, u32[]{:S(2)}, u32[]{:S(2)}) collective-permute-start(f32[8,1536]{1,0:T(8,128)S(1)} %fusion), channel_id=1, source_target_pairs={{0,3},{1,4},{2,5},{3,6},{4,7},{5,8},{6,9},{7,10},{8,11},{9,12},{10... | collective-permute-start | bytes 147464
  930.9 71.6 %collective-permute-start.13 = (f32[8,1536]{1,0:T(8,128)S(1)}, f32[8,1536]{1,0:T(8,128)S(1)}, u32[]{:S(2)}, u32[]{:S(2)}) collective-permute-start(f32[8,1536]{1,0:T(8,128)S(1)} %fusion), channel_id=1, source_target_pairs={{0,4},{1,5},{2,6},{3,7},{4,8},{5,9},{6,10},{7,11},{8,12},{9,13},{1... | collective-permute-start | bytes 147464
  944.0 71.6 %collective-permute-start.14 = (f32[8,1536]{1,0:T(8,128)S(1)}, f32[8,1536]{1,0:T(8,128)S(1)}, u32[]{:S(2)}, u32[]{:S(2)}) collective-permute-start(f32[8,1536]{1,0:T(8,128)S(1)} %fusion), channel_id=1, source_target_pairs={{0,5},{1,6},{2,7},{3,8},{4,9},{5,10},{6,11},{7,12},{8,13},{9,14},{... | collective-permute-start | bytes 147464
  957.2 71.7 %collective-permute-start.15 = (f32[8,1536]{1,0:T(8,128)S(1)}, f32[8,1536]{1,0:T(8,128)S(1)}, u32[]{:S(2)}, u32[]{:S(2)}) collective-permute-start(f32[8,1536]{1,0:T(8,128)S(1)} %fusion), channel_id=1, source_target_pairs={{0,6},{1,7},{2,8},{3,9},{4,10},{5,11},{6,12},{7,13},{8,14},{9,15},... | collective-permute-start | bytes 147464
  970.3 71.7 %collective-permute-start.16 = (f32[8,1536]{1,0:T(8,128)S(1)}, f32[8,1536]{1,0:T(8,128)S(1)}, u32[]{:S(2)}, u32[]{:S(2)}) collective-permute-start(f32[8,1536]{1,0:T(8,128)S(1)} %fusion), channel_id=1, source_target_pairs={{0,7},{1,8},{2,9},{3,10},{4,11},{5,12},{6,13},{7,14},{8,15},{9,16}... | collective-permute-start | bytes 147464
  989.4 69.4 %collective-permute-start.17 = (f32[8,1536]{1,0:T(8,128)S(1)}, f32[8,1536]{1,0:T(8,128)S(1)}, u32[]{:S(2)}, u32[]{:S(2)}) collective-permute-start(f32[8,1536]{1,0:T(8,128)S(1)} %fusion), channel_id=1, source_target_pairs={{0,8},{1,9},{2,10},{3,11},{4,12},{5,13},{6,14},{7,15},{8,16},{9,17... | collective-permute-start | bytes 147464
  1002.5 69.3 %collective-permute-start.18 = (f32[8,1536]{1,0:T(8,128)S(1)}, f32[8,1536]{1,0:T(8,128)S(1)}, u32[]{:S(2)}, u32[]{:S(2)}) collective-permute-start(f32[8,1536]{1,0:T(8,128)S(1)} %fusion), channel_id=1, source_target_pairs={{0,9},{1,10},{2,11},{3,12},{4,13},{5,14},{6,15},{7,16},{8,17},{9,1... | collective-permute-start | bytes 147464
  1085.0 69.9 %collective-permute-start.24 = (f32[8,1536]{1,0:T(8,128)S(1)}, f32[8,1536]{1,0:T(8,128)S(1)}, u32[]{:S(2)}, u32[]{:S(2)}) collective-permute-start(f32[8,1536]{1,0:T(8,128)S(1)} %fusion), channel_id=1, source_target_pairs={{0,15},{1,16},{2,17},{3,18},{4,19},{5,20},{6,21},{7,22},{8,23},{9,... | collective-permute-start | bytes 147464
  1098.2 69.9 %collective-permute-start.25 = (f32[8,1536]{1,0:T(8,128)S(1)}, f32[8,1536]{1,0:T(8,128)S(1)}, u32[]{:S(2)}, u32[]{:S(2)}) collective-permute-start(f32[8,1536]{1,0:T(8,128)S(1)} %fusion), channel_id=1, source_target_pairs={{0,16},{1,17},{2,18},{3,19},{4,20},{5,21},{6,22},{7,23},{8,24},{9,... | collective-permute-start | bytes 147464
  1111.3 69.9 %collective-permute-start.26 = (f32[8,1536]{1,0:T(8,128)S(1)}, f32[8,1536]{1,0:T(8,128)S(1)}, u32[]{:S(2)}, u32[]{:S(2)}) collective-permute-start(f32[8,1536]{1,0:T(8,128)S(1)} %fusion), channel_id=1, source_target_pairs={{0,17},{1,18},{2,19},{3,20},{4,21},{5,22},{6,23},{7,24},{8,25},{9,... | collective-permute-start | bytes 147464
  1128.1 72.5 %collective-permute-start.27 = (f32[8,1536]{1,0:T(8,128)S(1)}, f32[8,1536]{1,0:T(8,128)S(1)}, u32[]{:S(2)}, u32[]{:S(2)}) collective-permute-start(f32[8,1536]{1,0:T(8,128)S(1)} %fusion), channel_id=1, source_target_pairs={{0,18},{1,19},{2,20},{3,21},{4,22},{5,23},{6,24},{7,25},{8,26},{9,... | collective-permute-start | bytes 147464
  1141.2 72.0 %collective-permute-start.28 = (f32[8,1536]{1,0:T(8,128)S(1)}, f32[8,1536]{1,0:T(8,128)}, u32[]{:S(2)}, u32[]{:S(2)}) collective-permute-start(f32[8,1536]{1,0:T(8,128)S(1)} %fusion), channel_id=1, source_target_pairs={{0,19},{1,20},{2,21},{3,22},{4,23},{5,24},{6,25},{7,26},{8,27},{9,... | collective-permute-start | bytes 147464
  1154.9 71.4 %collective-permute-start.29 = (f32[8,1536]{1,0:T(8,128)S(1)}, f32[8,1536]{1,0:T(8,128)}, u32[]{:S(2)}, u32[]{:S(2)}) collective-permute-start(f32[8,1536]{1,0:T(8,128)S(1)} %fusion), channel_id=1, source_target_pairs={{0,20},{1,21},{2,22},{3,23},{4,24},{5,25},{6,26},{7,27},{8,28},{9,... | collective-permute-start | bytes 147464
  1168.1 71.4 %collective-permute-start.30 = (f32[8,1536]{1,0:T(8,128)S(1)}, f32[8,1536]{1,0:T(8,128)}, u32[]{:S(2)}, u32[]{:S(2)}) collective-permute-start(f32[8,1536]{1,0:T(8,128)S(1)} %fusion), channel_id=1, source_target_pairs={{0,21},{1,22},{2,23},{3,24},{4,25},{5,26},{6,27},{7,28},{8,29},{9,... | collective-permute-start | bytes 147464
  1181.2 71.4 %collective-permute-start.31 = (f32[8,1536]{1,0:T(8,128)S(1)}, f32[8,1536]{1,0:T(8,128)}, u32[]{:S(2)}, u32[]{:S(2)}) collective-permute-start(f32[8,1536]{1,0:T(8,128)S(1)} %fusion), channel_id=1, source_target_pairs={{0,22},{1,23},{2,24},{3,25},{4,26},{5,27},{6,28},{7,29},{8,30},{9,... | collective-permute-start | bytes 147464
  1267.5 103.1 %collective-permute-start.37 = (f32[8,1536]{1,0:T(8,128)S(1)}, f32[8,1536]{1,0:T(8,128)}, u32[]{:S(2)}, u32[]{:S(2)}) collective-permute-start(f32[8,1536]{1,0:T(8,128)S(1)} %fusion), channel_id=1, source_target_pairs={{0,28},{1,29},{2,30},{3,31},{4,32},{5,33},{6,34},{7,35},{8,36},{9,... | collective-permute-start | bytes 147464
  1281.2 98.0 %collective-permute-start.38 = (f32[8,1536]{1,0:T(8,128)S(1)}, f32[8,1536]{1,0:T(8,128)}, u32[]{:S(2)}, u32[]{:S(2)}) collective-permute-start(f32[8,1536]{1,0:T(8,128)S(1)} %fusion), channel_id=1, source_target_pairs={{0,29},{1,30},{2,31},{3,32},{4,33},{5,34},{6,35},{7,36},{8,37},{9,... | collective-permute-start | bytes 147464
  1294.4 87.9 %collective-permute-start.39 = (f32[8,1536]{1,0:T(8,128)S(1)}, f32[8,1536]{1,0:T(8,128)}, u32[]{:S(2)}, u32[]{:S(2)}) collective-permute-start(f32[8,1536]{1,0:T(8,128)S(1)} %fusion), channel_id=1, source_target_pairs={{0,30},{1,31},{2,32},{3,33},{4,34},{5,35},{6,36},{7,37},{8,38},{9,... | collective-permute-start | bytes 147464
  1307.5 84.3 %collective-permute-start.40 = (f32[8,1536]{1,0:T(8,128)S(1)}, f32[8,1536]{1,0:T(8,128)}, u32[]{:S(2)}, u32[]{:S(2)}) collective-permute-start(f32[8,1536]{1,0:T(8,128)S(1)} %fusion), channel_id=1, source_target_pairs={{0,31},{1,32},{2,33},{3,34},{4,35},{5,36},{6,37},{7,38},{8,39},{9,... | collective-permute-start | bytes 147464
  1315.9 78.8 %collective-permute-start.41 = (f32[8,1536]{1,0:T(8,128)S(1)}, f32[8,1536]{1,0:T(8,128)}, u32[]{:S(2)}, u32[]{:S(2)}) collective-permute-start(f32[8,1536]{1,0:T(8,128)S(1)} %fusion), channel_id=1, source_target_pairs={{0,32},{1,33},{2,34},{3,35},{4,36},{5,37},{6,38},{7,39},{8,40},{9,... | collective-permute-start | bytes 147464
  1466.4 252.4 %collective-permute-start.8 = (bf16[2,256,1536]{1,2,0:T(8,128)(2,1)}, bf16[2,256,1536]{1,2,0:T(8,128)(2,1)}, u32[]{:S(2)}, u32[]{:S(2)}) collective-permute-start(bf16[2,256,1536]{1,2,0:T(8,128)(2,1)} %pad_maximum_fusion.1), channel_id=1, source_target_pairs={{1,0},{2,1},{3,2},{4,3},{5,4},{6,5},{7,6},{8,7},{9,8},{10,9},{11,1... | collective-permute-start | bytes 4718600 | tf_op jit(solution)/shard_map/ppermute | solution.py:26
  1469.0 251.5 %collective-permute-start.9 = (bf16[2,256,1536]{1,2,0:T(8,128)(2,1)}, bf16[2,256,1536]{1,2,0:T(8,128)(2,1)}, u32[]{:S(2)}, u32[]{:S(2)}) collective-permute-start(bf16[2,256,1536]{1,2,0:T(8,128)(2,1)} %pad_maximum_fusion.2), channel_id=1, source_target_pairs={{0,1},{1,2},{2,3},{3,4},{4,5},{5,6},{6,7},{7,8},{8,9},{9,10},{10,1... | collective-permute-start | bytes 4718600 | tf_op jit(solution)/shard_map/ppermute | solution.py:26
  (209 other events, 11220.4 us)
Sparse Core Ops, SparseCore 0:
  1476.9 240.1 all-reduce.3
where the time goes:
time: 1750 us; the launch traced here: 1730 us
  blocking collectives  723 us (41%)
  starting transfers between devices  543 us (31%)
  local copies, waits for them, and re-layouts  176 us (10%)
  waiting for transfers between devices  133 us (8%)
  other arithmetic  95.4 us (5%)
  matrix products  43.9 us (3%)
  between operations  17.7 us (1%)
    unnamed x1, blocking collectives  723 us
    unnamed x64, starting transfers between devices  491 us
    psum x1, waiting for transfers between devices, per_device(): grad_kernel = lax.psum(jnp.stack(kernel_rows), ('dp', 'seq')) * scale_out  129 us
    unnamed x323, local copies, waits for them, and re-layouts  104 us
    reduce_sum x6, other arithmetic, per_device(): jnp.sum(jnp.where(masks[offset], conv_grad_f * attended_wide[offset:offse...  40.2 us
  transfers between devices with their start and end apart: 75, of which 3 were waited for; matrix products, arithmetic and copies ran while one was open for 11% of the time, Pallas kernels for 0%

commit v1 on v0

--- a/solution.py
+++ b/solution.py
@@ -145,7 +145,7 @@
             )
         )
     scale_out = (lax.axis_size("dp") * lax.axis_size("seq") * frame_count) ** (-0.5)
-    grad_kernel = lax.psum(jnp.stack(kernel_rows), ("dp", "seq")) * scale_out
+    grad_kernel = lax.psum(lax.psum(jnp.stack(kernel_rows), "seq"), "dp") * scale_out
     attended_grad_b = attended_grad.astype(jnp.bfloat16)
     reduced = lax.psum_scatter(
         lax.dot_general(

time: 1750 us -> 1780 us (1.017)
  waiting for transfers between devices: 133 us -> 162 us
    psum x1 -> x2, waiting for transfers between devices: 129 us -> 158 us  [the longest x1 158 us: per_device(): lax.psum(jnp.stack(kernel_rows), 'seq')]
    unnamed x323 -> x287, local copies, waits for them, and re-layouts: 104 us -> 109 us
  transfers between devices with their start and end apart: 75 -> 76, of which waited for: 3 -> 2; matrix products, arithmetic and copies ran while one was open for 11% -> 11% of each run, Pallas kernels for 0% -> 0%
where the time goes in v1:
time: 1780 us; the launch traced here: 1770 us
  blocking collectives  723 us (41%)
  starting transfers between devices  544 us (31%)
  local copies, waits for them, and re-layouts  183 us (10%)
  waiting for transfers between devices  162 us (9%)
  other arithmetic  94.3 us (5%)
  matrix products  44.3 us (2%)
    unnamed x1, blocking collectives  723 us
    unnamed x64, starting transfers between devices  491 us
    psum x1, waiting for transfers between devices, per_device(): lax.psum(jnp.stack(kernel_rows), 'seq')  158 us
    unnamed x287, local copies, waits for them, and re-layouts  109 us
    reduce_sum x6, other arithmetic, per_device(): jnp.sum(jnp.where(masks[offset], conv_grad_f * attended_wide[offset:offse...  40.1 us
  transfers between devices with their start and end apart: 76, of which 2 were waited for; matrix products, arithmetic and copies ran while one was open for 11% of the time, Pallas kernels for 0%

profile of v1, /device:TPU:1, one launch (start us, length us, event | category | flops | bytes accessed | tf_op | source)
XLA Modules:
  0.0 1768.2 jit_solution(8348227823383084855)
XLA Ops:
  8.6 15.1 collective-permute-start.1
  30.7 13.3 collective-permute-start.3
  60.6 40.0 %while.30 = (s32[]{:T(128)}, f32[6,256,256]{1,2,0:T(8,128)S(1)}, f32[6,4,256]{2,1,0:T(4,128)}, f32[6,4,256]{2,1,0:T(4,128)}, bf16[6,768,256]{1,2,0:T(8,128)(2,1)...) while((s32[]{:T(128)}, f32[6,256,256]{1,2,0:T(8,128)S(1)}, ...), condition=%wide.region_3.4_spmd.clone, body=%wide.region_0.3_spmd.sunk.clone | while | flops 210958336 | bytes 13804141 | solution.py:104
  114.4 22.6 %fusion.142 = (f32[1536]{0:T(1024)}, f32[1536]{0:T(1024)}, f32[1536]{0:T(1024)}, f32[1536]{0:T(1024)}, f32[1536]{0:T(1024)}, /*index=5*/f32[1536]{0:T(1024)}, bf16[256,1536]{1,0:T(8,128)(2,1)S(1)}, f32[256,1536]{1,0:T(8,128)}) fusion(pred[256]{0:T(512)(128)(4,1)S(1)} %get-tuple-element.289, bf16[15,1536]{1,0:T(8,128)(2,1)S(1)} %collective-permute-done.5, ...), kind=kLoop, calls=%fused_computation.286 | loop fusion | flops 104193024 | bytes 4259328 | tf_op jit(solution)/shard_map/reduce_sum | solution.py:138
  145.0 24.2 %fusion.149 = bf16[256,1536]{1,0:T(8,128)(2,1)S(1)} fusion(bf16[256,1536]{1,0:T(8,128)(2,1)S(1)} %get-tuple-element.248, bf16[15,1536]{1,0:T(8,128)(2,1)} %collective-permute-done.7, bf16[15,1536]{1,0:T(8,128)(2,1)} %copy-done.56, f32[1536]{0:T(1024)S(1)} %get-tuple-element.174, f32[1536]{0:T(1024)S(1)} %get-tuple-element.175, ...), kind=kLoop, calls=%fused_computation.304 | loop fusion | flops 83755008 | bytes 1863168 | tf_op jit(solution)/shard_map/convert_element_type | solution.py:149
  174.2 723.2 %fusion = f32[8,1536]{1,0:T(8,128)S(1)} fusion(f32[1536,1536]{1,0:T(8,128)} %fusion.216), kind=kCustom, calls=%all-reduce-scatter | all-reduce-scatter fusion | flops 3145729 | bytes 9486336
  899.9 13.3 collective-permute-start.11
  933.1 13.1 collective-permute-start.13
  946.2 13.1 collective-permute-start.14
  959.3 13.1 collective-permute-start.15
  972.5 13.1 collective-permute-start.16
  1004.7 13.1 collective-permute-start.18
  1017.9 13.1 collective-permute-start.19
  1114.2 13.3 collective-permute-start.26
  1144.0 13.7 collective-permute-start.28
  1157.8 13.2 collective-permute-start.29
  1170.9 13.1 collective-permute-start.30
  1184.7 13.1 collective-permute-start.31
  1270.8 13.7 collective-permute-start.37
  1284.6 13.2 collective-permute-start.38
  1297.7 13.1 collective-permute-start.39
  1321.5 52.4 %while.31 = (s32[]{:T(128)}, bf16[6,256,256]{1,2,0:T(8,128)(2,1)S(1)}, f32[6,768,256]{1,2,0:T(8,128)}, f32[6,768,256]{1,2,0:T(8,128)}, bf16[6,768,256]{1,2,0:T(8...) while((s32[]{:T(128)}, ...), condition=%wide.region_6.7_spmd.clone, body=%wide.region_5.6_spmd.sunk.clone | while | flops 510590976 | bytes 23504016 | solution.py:174
  1492.9 158.4 %all-reduce.5.cloned.1.call-done = f32[31,1536]{1,0:T(8,128)} async-done(((f32[31,1536]{1,0:T(8,128)}), f32[31,1536]{1,0:T(8,128)}) %all-reduce.5.cloned.1.call-update) | async-done | bytes 190480 | tf_op jit(solution)/shard_map/psum | solution.py:148
  1651.4 97.5 %concatenate.118 = f32[518,1536]{1,0:T(8,128)} concatenate(f32[6,1536]{1,0:T(8,128)S(1)} %collective-permute-done.73, f32[8,1536]{1,0:T(8,128)} %collective-permute-done.72, f32[8,1536]{1,0:T(8,128)} %collective-permute-done.71, f32[8,1536]{1,0:T(8,128)} %collective-permute-done.70, f32[8,1536]{1,0:T(8,128)} %collective-permute-done.69, f32[8,1536]{1,0:T(8,128)} %collective-permute-done.68, ...), dimensions={0} | concatenate | bytes 6365184
  (631 shorter events, 497.4 us)
Async XLA Ops:
  7.2 1644.1 %all-reduce.5.cloned.1.call-start = ((), (), s32[]{:S(2)}) async-start(), calls=%async_computation | async-start | bytes 393216 | tf_op jit(solution)/shard_map/psum | solution.py:148
  899.9 72.5 %collective-permute-start.11 = (f32[8,1536]{1,0:T(8,128)S(1)}, f32[8,1536]{1,0:T(8,128)S(1)}, u32[]{:S(2)}, u32[]{:S(2)}) collective-permute-start(f32[8,1536]{1,0:T(8,128)S(1)} %fusion), channel_id=1, source_target_pairs={{0,2},{1,3},{2,4},{3,5},{4,6},{5,7},{6,8},{7,9},{8,10},{9,11},{10,... | collective-permute-start | bytes 147464
  920.0 71.6 %collective-permute-start.12 = (f32[8,1536]{1,0:T(8,128)S(1)}, f32[8,1536]{1,0:T(8,128)S(1)}, u32[]{:S(2)}, u32[]{:S(2)}) collective-permute-start(f32[8,1536]{1,0:T(8,128)S(1)} %fusion), channel_id=1, source_target_pairs={{0,3},{1,4},{2,5},{3,6},{4,7},{5,8},{6,9},{7,10},{8,11},{9,12},{10... | collective-permute-start | bytes 147464
  933.1 71.7 %collective-permute-start.13 = (f32[8,1536]{1,0:T(8,128)S(1)}, f32[8,1536]{1,0:T(8,128)S(1)}, u32[]{:S(2)}, u32[]{:S(2)}) collective-permute-start(f32[8,1536]{1,0:T(8,128)S(1)} %fusion), channel_id=1, source_target_pairs={{0,4},{1,5},{2,6},{3,7},{4,8},{5,9},{6,10},{7,11},{8,12},{9,13},{1... | collective-permute-start | bytes 147464
  946.2 71.7 %collective-permute-start.14 = (f32[8,1536]{1,0:T(8,128)S(1)}, f32[8,1536]{1,0:T(8,128)S(1)}, u32[]{:S(2)}, u32[]{:S(2)}) collective-permute-start(f32[8,1536]{1,0:T(8,128)S(1)} %fusion), channel_id=1, source_target_pairs={{0,5},{1,6},{2,7},{3,8},{4,9},{5,10},{6,11},{7,12},{8,13},{9,14},{... | collective-permute-start | bytes 147464
  959.3 71.7 %collective-permute-start.15 = (f32[8,1536]{1,0:T(8,128)S(1)}, f32[8,1536]{1,0:T(8,128)S(1)}, u32[]{:S(2)}, u32[]{:S(2)}) collective-permute-start(f32[8,1536]{1,0:T(8,128)S(1)} %fusion), channel_id=1, source_target_pairs={{0,6},{1,7},{2,8},{3,9},{4,10},{5,11},{6,12},{7,13},{8,14},{9,15},... | collective-permute-start | bytes 147464
  972.5 71.7 %collective-permute-start.16 = (f32[8,1536]{1,0:T(8,128)S(1)}, f32[8,1536]{1,0:T(8,128)S(1)}, u32[]{:S(2)}, u32[]{:S(2)}) collective-permute-start(f32[8,1536]{1,0:T(8,128)S(1)} %fusion), channel_id=1, source_target_pairs={{0,7},{1,8},{2,9},{3,10},{4,11},{5,12},{6,13},{7,14},{8,15},{9,16}... | collective-permute-start | bytes 147464
  1100.4 70.5 %collective-permute-start.25 = (f32[8,1536]{1,0:T(8,128)S(1)}, f32[8,1536]{1,0:T(8,128)S(1)}, u32[]{:S(2)}, u32[]{:S(2)}) collective-permute-start(f32[8,1536]{1,0:T(8,128)S(1)} %fusion), channel_id=1, source_target_pairs={{0,16},{1,17},{2,18},{3,19},{4,20},{5,21},{6,22},{7,23},{8,24},{9,... | collective-permute-start | bytes 147464
  1130.9 73.0 %collective-permute-start.27 = (f32[8,1536]{1,0:T(8,128)S(1)}, f32[8,1536]{1,0:T(8,128)S(1)}, u32[]{:S(2)}, u32[]{:S(2)}) collective-permute-start(f32[8,1536]{1,0:T(8,128)S(1)} %fusion), channel_id=1, source_target_pairs={{0,18},{1,19},{2,20},{3,21},{4,22},{5,23},{6,24},{7,25},{8,26},{9,... | collective-permute-start | bytes 147464
  1144.0 72.6 %collective-permute-start.28 = (f32[8,1536]{1,0:T(8,128)S(1)}, f32[8,1536]{1,0:T(8,128)}, u32[]{:S(2)}, u32[]{:S(2)}) collective-permute-start(f32[8,1536]{1,0:T(8,128)S(1)} %fusion), channel_id=1, source_target_pairs={{0,19},{1,20},{2,21},{3,22},{4,23},{5,24},{6,25},{7,26},{8,27},{9,... | collective-permute-start | bytes 147464
  1157.8 72.0 %collective-permute-start.29 = (f32[8,1536]{1,0:T(8,128)S(1)}, f32[8,1536]{1,0:T(8,128)}, u32[]{:S(2)}, u32[]{:S(2)}) collective-permute-start(f32[8,1536]{1,0:T(8,128)S(1)} %fusion), channel_id=1, source_target_pairs={{0,20},{1,21},{2,22},{3,23},{4,24},{5,25},{6,26},{7,27},{8,28},{9,... | collective-permute-start | bytes 147464
  1170.9 71.9 %collective-permute-start.30 = (f32[8,1536]{1,0:T(8,128)S(1)}, f32[8,1536]{1,0:T(8,128)}, u32[]{:S(2)}, u32[]{:S(2)}) collective-permute-start(f32[8,1536]{1,0:T(8,128)S(1)} %fusion), channel_id=1, source_target_pairs={{0,21},{1,22},{2,23},{3,24},{4,25},{5,26},{6,27},{7,28},{8,29},{9,... | collective-permute-start | bytes 147464
  1184.7 71.3 %collective-permute-start.31 = (f32[8,1536]{1,0:T(8,128)S(1)}, f32[8,1536]{1,0:T(8,128)}, u32[]{:S(2)}, u32[]{:S(2)}) collective-permute-start(f32[8,1536]{1,0:T(8,128)S(1)} %fusion), channel_id=1, source_target_pairs={{0,22},{1,23},{2,24},{3,25},{4,26},{5,27},{6,28},{7,29},{8,30},{9,... | collective-permute-start | bytes 147464
  1270.8 103.1 %collective-permute-start.37 = (f32[8,1536]{1,0:T(8,128)S(1)}, f32[8,1536]{1,0:T(8,128)}, u32[]{:S(2)}, u32[]{:S(2)}) collective-permute-start(f32[8,1536]{1,0:T(8,128)S(1)} %fusion), channel_id=1, source_target_pairs={{0,28},{1,29},{2,30},{3,31},{4,32},{5,33},{6,34},{7,35},{8,36},{9,... | collective-permute-start | bytes 147464
  1284.6 98.0 %collective-permute-start.38 = (f32[8,1536]{1,0:T(8,128)S(1)}, f32[8,1536]{1,0:T(8,128)}, u32[]{:S(2)}, u32[]{:S(2)}) collective-permute-start(f32[8,1536]{1,0:T(8,128)S(1)} %fusion), channel_id=1, source_target_pairs={{0,29},{1,30},{2,31},{3,32},{4,33},{5,34},{6,35},{7,36},{8,37},{9,... | collective-permute-start | bytes 147464
  1297.7 87.9 %collective-permute-start.39 = (f32[8,1536]{1,0:T(8,128)S(1)}, f32[8,1536]{1,0:T(8,128)}, u32[]{:S(2)}, u32[]{:S(2)}) collective-permute-start(f32[8,1536]{1,0:T(8,128)S(1)} %fusion), channel_id=1, source_target_pairs={{0,30},{1,31},{2,32},{3,33},{4,34},{5,35},{6,36},{7,37},{8,38},{9,... | collective-permute-start | bytes 147464
  1310.9 84.3 %collective-permute-start.40 = (f32[8,1536]{1,0:T(8,128)S(1)}, f32[8,1536]{1,0:T(8,128)}, u32[]{:S(2)}, u32[]{:S(2)}) collective-permute-start(f32[8,1536]{1,0:T(8,128)S(1)} %fusion), channel_id=1, source_target_pairs={{0,31},{1,32},{2,33},{3,34},{4,35},{5,36},{6,37},{7,38},{8,39},{9,... | collective-permute-start | bytes 147464
  1319.3 78.8 %collective-permute-start.41 = (f32[8,1536]{1,0:T(8,128)S(1)}, f32[8,1536]{1,0:T(8,128)}, u32[]{:S(2)}, u32[]{:S(2)}) collective-permute-start(f32[8,1536]{1,0:T(8,128)S(1)} %fusion), channel_id=1, source_target_pairs={{0,32},{1,33},{2,34},{3,35},{4,36},{5,37},{6,38},{7,39},{8,40},{9,... | collective-permute-start | bytes 147464
  1469.4 282.6 %collective-permute-start.8 = (bf16[2,256,1536]{1,2,0:T(8,128)(2,1)}, bf16[2,256,1536]{1,2,0:T(8,128)(2,1)}, u32[]{:S(2)}, u32[]{:S(2)}) collective-permute-start(bf16[2,256,1536]{1,2,0:T(8,128)(2,1)} %pad_maximum_fusion.1), channel_id=1, source_target_pairs={{1,0},{2,1},{3,2},{4,3},{5,4},{6,5},{7,6},{8,7},{9,8},{10,9},{11,1... | collective-permute-start | bytes 4718600 | tf_op jit(solution)/shard_map/ppermute | solution.py:26
  1471.8 281.9 %collective-permute-start.9 = (bf16[2,256,1536]{1,2,0:T(8,128)(2,1)}, bf16[2,256,1536]{1,2,0:T(8,128)(2,1)}, u32[]{:S(2)}, u32[]{:S(2)}) collective-permute-start(bf16[2,256,1536]{1,2,0:T(8,128)(2,1)} %pad_maximum_fusion.2), channel_id=1, source_target_pairs={{0,1},{1,2},{2,3},{3,4},{4,5},{5,6},{6,7},{7,8},{8,9},{9,10},{10,1... | collective-permute-start | bytes 4718600 | tf_op jit(solution)/shard_map/ppermute | solution.py:26
  1479.9 270.6 %all-reduce.7.cloned.1.call-start = ((), (), s32[]{:S(2)}) async-start(), calls=%async_computation.1 | async-start | bytes 393216 | tf_op jit(solution)/shard_map/psum | solution.py:148
  1479.9 171.4 %collective-permute-start.70 = (f32[8,1536]{1,0:T(8,128)S(1)}, f32[8,1536]{1,0:T(8,128)}, u32[]{:S(2)}, u32[]{:S(2)}) collective-permute-start(f32[8,1536]{1,0:T(8,128)S(1)} %fusion), channel_id=1, source_target_pairs={{0,61},{1,62},{2,63},{3,64},{4,65},{5,66},{6,67},{7,68},{8,69},{9,... | collective-permute-start | bytes 147464
  1482.1 169.2 %collective-permute-start.71 = (f32[8,1536]{1,0:T(8,128)S(1)}, f32[8,1536]{1,0:T(8,128)}, u32[]{:S(2)}, u32[]{:S(2)}) collective-permute-start(f32[8,1536]{1,0:T(8,128)S(1)} %fusion), channel_id=1, source_target_pairs={{0,62},{1,63},{2,64},{3,65},{4,66},{5,67},{6,68},{7,69},{8,70},{9,... | collective-permute-start | bytes 147464
  1484.0 167.3 %collective-permute-start.72 = (f32[8,1536]{1,0:T(8,128)S(1)}, f32[8,1536]{1,0:T(8,128)}, u32[]{:S(2)}, u32[]{:S(2)}) collective-permute-start(f32[8,1536]{1,0:T(8,128)S(1)} %fusion), channel_id=1, source_target_pairs={{0,63},{1,64},{2,65},{3,66},{4,67},{5,68},{6,69},{7,70},{8,71},{9,... | collective-permute-start | bytes 147464
  (192 other events, 11601.0 us)
Sparse Core Ops, SparseCore 0:
  1480.0 171.2 all-reduce.4
  1653.6 44.7 all-reduce.6
